TPU v7x, 256 devices: a whole 4x4x8 slice. The times are simulated.
256 devices in a mesh: wide: 32 (over z, x), narrow: 8 (over y, core).
Axes of the slice: x: 4, y: 4, z: 8, core: 2. Of those that a mesh axis runs over, the one named last changes fastest.
Arguments:
- data: bfloat16 [65536, 16384], P(('wide', 'narrow')), may hold values from -54 to 54, as said below
- players: float32 [64, 16384], P('narrow', 'wide'), may hold values from -0.046875 to 0.046875
Outputs:
- rescaled: float32 [64, 16384], P('narrow', 'wide')
Inputs may be any that keep to these rules, and one draw needn't show every extreme that they name: data rows with feature and row scales of their own.
All inputs are finite; a program needn't handle non-finite values.
Results may differ from a plain program's by a relative error of at most 0.012.
Values may be sent and summed in bfloat16 or wider, within the bound.
A program may use at most 64 MiB of HBM per device.

v0:
```python
import jax
import jax.numpy as jnp
from jax import lax
from jax.sharding import PartitionSpec as P

STEPS = 3


step_size = 0.5
epsilon = 1e-06


def on_device(data, players):
    block = players.shape[0]
    width = data.shape[1]
    count = block * lax.axis_size("narrow")
    nrows = data.shape[0] * lax.axis_size("wide") * lax.axis_size("narrow")
    owner = lax.axis_index("narrow")
    component = owner * block + jnp.arange(block)[:, None]
    later = jnp.arange(count)[None, :] < component
    v = players
    for step in range(STEPS):
        everyone = lax.all_gather(v, "narrow", axis=0, tiled=True)
        low = everyone.astype(jnp.bfloat16)
        proj = lax.dot_general(
            data,
            lax.all_gather(low, "wide", axis=1, tiled=True),
            (((1,), (1,)), ((), ())),
            preferred_element_type=jnp.float32,
        ).astype(jnp.bfloat16)
        partial_rows = lax.psum_scatter(
            lax.dot_general(
                proj, data, (((0,), (0,)), ((), ())), preferred_element_type=jnp.float32
            )
            / jnp.float32(nrows),
            "narrow",
            scatter_dimension=0,
            tiled=True,
        )
        moved = lax.psum_scatter(partial_rows, "wide", scatter_dimension=1, tiled=True)
        gram_local = lax.dot_general(
            moved, everyone, (((1,), (1,)), ((), ())), precision=lax.Precision.HIGHEST
        )
        gram = lax.psum(gram_local, "wide")
        weights = jnp.where(later, gram, jnp.float32(0.0))
        delta = moved - jnp.dot(weights, everyone, precision=lax.Precision.HIGHEST)
        align = lax.psum(jnp.sum(v * delta, axis=1), "wide")[:, None]
        upd = v + step_size * (delta - align * v)
        length = lax.psum(jnp.sum(upd * upd, axis=1), "wide")[:, None]
        v = upd * lax.rsqrt(length + epsilon)
    return v * jnp.float32(width) ** 0.5


def solution(mesh):
    placed = (P(("wide", "narrow"), None), P("narrow", "wide"))
    return jax.shard_map(
        on_device, mesh=mesh, in_specs=placed, out_specs=P("narrow", "wide"), check_vma=False
    )
```

profile of v0, /device:TPU:8, one launch (start us, length us, event | category | flops | bytes accessed | tf_op | source)
XLA Modules:
  0.0 1733.0 jit_solution(15584215705588049480)
XLA Ops:
  6.5 13.2 all_gather.18
  20.4 77.4 %all-gather.4.cloned.1.call-done = bf16[64,16384]{1,0:T(8,128)(2,1)} async-done(((bf16[64,512]{1,0:T(8,128)(2,1)}), bf16[64,16384]{1,0:T(8,128)(2,1)}) %all-gather.4.cloned.1.call-update) | async-done | bytes 2097168 | tf_op jit(solution)/shard_map/all_gather | solution.py:27
  97.8 14.2 convolution_multiply_fusion.2
  112.1 36.3 %reduce-scatter.7.cloned.1.call-done = f32[8,16384]{1,0:T(8,128)} async-done(((f32[64,16384]{1,0:T(8,128)}), f32[8,16384]{1,0:T(8,128)}) %reduce-scatter.7.cloned.1.call-update) | async-done | bytes 524304 | tf_op jit(solution)/shard_map/reduce_scatter | solution.py:31
  148.5 219.0 %reduce-scatter.9.cloned.1.call-done = f32[8,512]{1,0:T(8,128)} async-done(((f32[8,16384]{1,0:T(8,128)}), f32[8,512]{1,0:T(8,128)}) %reduce-scatter.9.cloned.1.call-update) | async-done | bytes 16400 | tf_op jit(solution)/shard_map/reduce_scatter | solution.py:40
  368.4 72.3 %psum.63 = f32[8,64]{1,0:T(8,128)S(1)} all-reduce(f32[8,64]{1,0:T(8,128)S(1)} %fusion.12), channel_id=1, replica_groups=mesh['wide'=32,'narrow'=8] {'wide'}, use_global_device_ids=true, to_apply=%region_2.0 | all-reduce | flops 512 | bytes 4096 | tf_op jit(solution)/shard_map/psum | solution.py:44
  441.7 69.6 %psum.64 = f32[8]{0:T(128)S(1)} all-reduce(f32[8]{0:T(128)S(1)} %get-tuple-element.5), channel_id=1, replica_groups=mesh['wide'=32,'narrow'=8] {'wide'}, use_global_device_ids=true, to_apply=%region_4.5 | all-reduce | flops 8 | bytes 64 | tf_op jit(solution)/shard_map/psum | solution.py:47
  511.5 71.7 %psum.65 = f32[8]{0:T(128)S(1)} all-reduce(f32[8]{0:T(128)S(1)} %multiply_reduce_fusion.4), channel_id=1, replica_groups=mesh['wide'=32,'narrow'=8] {'wide'}, use_global_device_ids=true, to_apply=%region_6.7 | all-reduce | flops 8 | bytes 64 | tf_op jit(solution)/shard_map/psum | solution.py:49
  583.3 12.8 all_gather.20
  596.8 72.1 %all-gather.6.cloned.1.call-done = bf16[64,16384]{1,0:T(8,128)(2,1)} async-done(((bf16[64,512]{1,0:T(8,128)(2,1)}), bf16[64,16384]{1,0:T(8,128)(2,1)}) %all-gather.6.cloned.1.call-update) | async-done | bytes 2097168 | tf_op jit(solution)/shard_map/all_gather | solution.py:27
  668.8 14.2 convolution_multiply_fusion.1
  683.0 36.2 %reduce-scatter.11.cloned.1.call-done = f32[8,16384]{1,0:T(8,128)} async-done(((f32[64,16384]{1,0:T(8,128)}), f32[8,16384]{1,0:T(8,128)}) %reduce-scatter.11.cloned.1.call-update) | async-done | bytes 524304 | tf_op jit(solution)/shard_map/reduce_scatter | solution.py:31
  719.3 219.5 %reduce-scatter.13.cloned.1.call-done = f32[8,512]{1,0:T(8,128)} async-done(((f32[8,16384]{1,0:T(8,128)}), f32[8,512]{1,0:T(8,128)}) %reduce-scatter.13.cloned.1.call-update) | async-done | bytes 16400 | tf_op jit(solution)/shard_map/reduce_scatter | solution.py:40
  939.8 72.3 %psum.66 = f32[8,64]{1,0:T(8,128)S(1)} all-reduce(f32[8,64]{1,0:T(8,128)S(1)} %fusion.13), channel_id=1, replica_groups=mesh['wide'=32,'narrow'=8] {'wide'}, use_global_device_ids=true, to_apply=%region_9.10 | all-reduce | flops 512 | bytes 4096 | tf_op jit(solution)/shard_map/psum | solution.py:44
  1013.1 69.6 %psum.67 = f32[8]{0:T(128)S(1)} all-reduce(f32[8]{0:T(128)S(1)} %get-tuple-element.7), channel_id=1, replica_groups=mesh['wide'=32,'narrow'=8] {'wide'}, use_global_device_ids=true, to_apply=%region_11.12 | all-reduce | flops 8 | bytes 64 | tf_op jit(solution)/shard_map/psum | solution.py:47
  1083.0 71.7 %psum.68 = f32[8]{0:T(128)S(1)} all-reduce(f32[8]{0:T(128)S(1)} %multiply_reduce_fusion.2), channel_id=1, replica_groups=mesh['wide'=32,'narrow'=8] {'wide'}, use_global_device_ids=true, to_apply=%region_13.14 | all-reduce | flops 8 | bytes 64 | tf_op jit(solution)/shard_map/psum | solution.py:49
  1154.7 13.0 all_gather.22
  1168.4 72.0 %all-gather.8.cloned.1.call-done = bf16[64,16384]{1,0:T(8,128)(2,1)} async-done(((bf16[64,512]{1,0:T(8,128)(2,1)}), bf16[64,16384]{1,0:T(8,128)(2,1)}) %all-gather.8.cloned.1.call-update) | async-done | bytes 2097168 | tf_op jit(solution)/shard_map/all_gather | solution.py:27
  1240.4 14.2 convolution_multiply_fusion
  1254.6 36.2 %reduce-scatter.15.cloned.1.call-done = f32[8,16384]{1,0:T(8,128)} async-done(((f32[64,16384]{1,0:T(8,128)}), f32[8,16384]{1,0:T(8,128)}) %reduce-scatter.15.cloned.1.call-update) | async-done | bytes 524304 | tf_op jit(solution)/shard_map/reduce_scatter | solution.py:31
  1290.9 219.1 %reduce-scatter.17.cloned.1.call-done = f32[8,512]{1,0:T(8,128)} async-done(((f32[8,16384]{1,0:T(8,128)}), f32[8,512]{1,0:T(8,128)}) %reduce-scatter.17.cloned.1.call-update) | async-done | bytes 16400 | tf_op jit(solution)/shard_map/reduce_scatter | solution.py:40
  1510.9 72.3 %psum.69 = f32[8,64]{1,0:T(8,128)S(1)} all-reduce(f32[8,64]{1,0:T(8,128)S(1)} %fusion.14), channel_id=1, replica_groups=mesh['wide'=32,'narrow'=8] {'wide'}, use_global_device_ids=true, to_apply=%region_16.17 | all-reduce | flops 512 | bytes 4096 | tf_op jit(solution)/shard_map/psum | solution.py:44
  1584.3 69.6 %psum.70 = f32[8]{0:T(128)S(1)} all-reduce(f32[8]{0:T(128)S(1)} %get-tuple-element.9), channel_id=1, replica_groups=mesh['wide'=32,'narrow'=8] {'wide'}, use_global_device_ids=true, to_apply=%region_18.19 | all-reduce | flops 8 | bytes 64 | tf_op jit(solution)/shard_map/psum | solution.py:47
  1654.1 71.7 %psum.71 = f32[8]{0:T(128)S(1)} all-reduce(f32[8]{0:T(128)S(1)} %multiply_reduce_fusion), channel_id=1, replica_groups=mesh['wide'=32,'narrow'=8] {'wide'}, use_global_device_ids=true, to_apply=%region_20.21 | all-reduce | flops 8 | bytes 64 | tf_op jit(solution)/shard_map/psum | solution.py:49
  (39 shorter events, 9.6 us)
Async XLA Ops:
  6.5 91.2 %all-gather.4.cloned.1.call-start = ((), (), s32[]{:S(2)}) async-start(), calls=%async_computation.6 | async-start | bytes 2162688 | tf_op jit(solution)/shard_map/all_gather | solution.py:27
  20.4 128.0 %reduce-scatter.7.cloned.1.call-start = ((), (), s32[]{:S(2)}) async-start(), calls=%async_computation.7 | async-start | bytes 4718592 | tf_op jit(solution)/shard_map/reduce_scatter | solution.py:31
  112.0 328.7 %copy-start = (f32[8,512]{1,0:T(8,128)S(1)}, f32[8,512]{1,0:T(8,128)}, u32[]{:S(2)}) copy-start(f32[8,512]{1,0:T(8,128)} %param.3) | copy-start | bytes 49156
  112.0 255.5 %reduce-scatter.9.cloned.1.call-start = ((), (), s32[]{:S(2)}) async-start(), calls=%async_computation.8 | async-start | bytes 540672 | tf_op jit(solution)/shard_map/reduce_scatter | solution.py:40
  148.4 520.4 %all-gather.6.cloned.1.call-start = ((), (), s32[]{:S(2)}) async-start(), calls=%async_computation.9 | async-start | bytes 2162688 | tf_op jit(solution)/shard_map/all_gather | solution.py:27
  596.7 122.6 %reduce-scatter.11.cloned.1.call-start = ((), (), s32[]{:S(2)}) async-start(), calls=%async_computation.10 | async-start | bytes 4718592 | tf_op jit(solution)/shard_map/reduce_scatter | solution.py:31
  683.0 255.9 %reduce-scatter.13.cloned.1.call-start = ((), (), s32[]{:S(2)}) async-start(), calls=%async_computation.11 | async-start | bytes 540672 | tf_op jit(solution)/shard_map/reduce_scatter | solution.py:40
  719.3 521.1 %all-gather.8.cloned.1.call-start = ((), (), s32[]{:S(2)}) async-start(), calls=%async_computation.12 | async-start | bytes 2162688 | tf_op jit(solution)/shard_map/all_gather | solution.py:27
  1168.3 122.5 %reduce-scatter.15.cloned.1.call-start = ((), (), s32[]{:S(2)}) async-start(), calls=%async_computation.13 | async-start | bytes 4718592 | tf_op jit(solution)/shard_map/reduce_scatter | solution.py:31
  1254.6 255.4 %reduce-scatter.17.cloned.1.call-start = ((), (), s32[]{:S(2)}) async-start(), calls=%async_computation.14 | async-start | bytes 540672 | tf_op jit(solution)/shard_map/reduce_scatter | solution.py:40
Sparse Core Ops, SparseCore 0:
  20.5 77.2 all-gather.3
  112.2 36.1 reduce-scatter.6
  152.2 215.2 reduce-scatter.8
  596.8 71.9 all-gather.5
  683.1 36.1 reduce-scatter.10
  723.4 215.4 reduce-scatter.12
  1168.4 71.9 all-gather.7
  1254.7 36.1 reduce-scatter.14
  1294.7 215.3 reduce-scatter.16
where the time goes:
time: 1730 us
  waiting for transfers between devices  988 us (57%)
  blocking collectives  680 us (39%)
  matrix products  48.4 us (3%)
    reduce_scatter x3, waiting for transfers between devices, on_device(): lax.psum_scatter(partial_rows, 'wide', scatter_dimension=1, tiled=True)  658 us
    all_gather x3, waiting for transfers between devices, on_device(): lax.all_gather(low, 'wide', axis=1, tiled=True)  221 us
    psum x3, blocking collectives, on_device(): gram = lax.psum(gram_local, 'wide')  217 us
    psum x3, blocking collectives, on_device(): length = lax.psum(jnp.sum(upd * upd, axis=1), 'wide')[:, None]  215 us
    psum x3, blocking collectives, on_device(): align = lax.psum(jnp.sum(v * delta, axis=1), 'wide')[:, None]  209 us
    reduce_scatter x3, waiting for transfers between devices, on_device(): lax.psum_scatter(lax.dot_general(proj, data, (((0,), (0,)), ((), ())), pr...  109 us
    dot_general x3, matrix products, on_device(): lax.dot_general(proj, data, (((0,), (0,)), ((), ())), preferred_element_t...  42.6 us
    all_gather x3, blocking collectives, on_device(): everyone = lax.all_gather(v, 'narrow', axis=0, tiled=True)  38.9 us
  transfers between devices with their start and end apart: 9, of which 9 were waited for; matrix products, arithmetic and copies ran while one was open for 0% of the time, Pallas kernels for 0%

commit v1 on v0

v1 whole, which is shorter than its diff:
```python
import functools

import jax
import jax.numpy as jnp
from jax import lax
from jax.experimental import pallas as pl
from jax.experimental.pallas import tpu as pltpu
from jax.sharding import PartitionSpec as P

STEPS = 3
step_size = 0.5
epsilon = 1e-06

X = 4
Y = 4
ROWS = 16
LANES = 128

MESH = pl.DeviceIdType.MESH
F32 = jnp.float32
BF16 = jnp.bfloat16


def exact(a, b, contract=((1,), (0,))):
    return lax.dot_general(
        a, b, (contract, ((), ())), precision=lax.Precision.HIGHEST, preferred_element_type=F32
    )


def nt(a, b):
    return lax.dot_general(a, b, (((1,), (1,)), ((), ())), preferred_element_type=F32)


def kernel(
    Z,
    nrows,
    data_hbm,
    players_ref,
    out_ref,
    data_v,
    basis,
    pair_send,
    pair_recv,
    own,
    s1_send,
    s1a_recv,
    s1b_recv,
    s2_send,
    s2_recv,
    s3_send,
    s3_recv,
    players_recv,
    rows_v,
    data_sem,
    send_sem,
    first_recv_sem,
    ag_recv_sem,
    ag_core_sem,
    rs_core_sem,
    rs1a_sem,
    rs1b_sem,
    rs2_sem,
    rs3_sem,
):
    wide = lax.axis_index("wide")
    narrow = lax.axis_index("narrow")
    z, x = wide // X, wide % X
    y, c = narrow // 2, narrow % 2
    o = 1 - c
    count = Y * ROWS
    span = Z * LANES
    depth = data_v.shape[0]

    def at_x(d):
        return (z * X + lax.rem(x + d, X), narrow)

    def at_y(d):
        return (wide, lax.rem(y + d, Y) * 2 + c)

    def at_z(d):
        return (lax.rem(z + d, Z) * X + x, narrow)

    sibling = (wide, y * 2 + o)

    def xlanes(xq):
        return pl.ds(pl.multiple_of(xq * span, span), span)

    def yrows(yq):
        return pl.ds(pl.multiple_of(yq * ROWS, ROWS), ROWS)

    def zlanes(zq):
        return pl.ds(pl.multiple_of(zq * LANES, LANES), LANES)

    def lanes(xq, zq):
        return pl.ds(pl.multiple_of((xq * Z + zq) * LANES, LANES), LANES)

    def columns(xq, zq, cq):
        return pl.ds(pl.multiple_of(((zq * X + xq) * 2 + cq) * 2 * LANES, 2 * LANES), 2 * LANES)

    pending = []

    def send(src, dst, ssem, rsem, where):
        copy = pltpu.make_async_remote_copy(
            src_ref=src, dst_ref=dst, send_sem=ssem, recv_sem=rsem, device_id=where, device_id_type=MESH
        )
        copy.start()
        return copy

    def wait_for(ref, sem):
        pltpu.make_async_copy(ref, ref, sem).wait()

    load = pltpu.make_async_copy(data_hbm, data_v, data_sem)
    load.start()

    barrier = pltpu.get_barrier_semaphore()
    peers = [sibling]
    peers += [at_x(d) for d in range(1, X)]
    peers += [at_y(d) for d in range(1, Y)]
    peers += [at_z(d) for d in range(1, Z)]
    for peer in peers:
        pl.semaphore_signal(barrier, inc=1, device_id=peer, device_id_type=MESH)
    pl.semaphore_wait(barrier, len(peers))

    first = send(
        players_ref.at[:, pl.ds(pl.multiple_of(o * 2 * LANES, 2 * LANES), 2 * LANES)],
        players_recv,
        send_sem.at[0],
        first_recv_sem,
        sibling,
    )
    first.wait()
    mine = players_ref[:, pl.ds(pl.multiple_of(c * 2 * LANES, 2 * LANES), 2 * LANES)]
    theirs = players_recv[...]
    block = jnp.where(
        c == 0, jnp.concatenate([mine, theirs], axis=0), jnp.concatenate([theirs, mine], axis=0)
    ).astype(BF16)
    for p in range(2):
        basis[0, c, p, yrows(y), lanes(x, z)] = block[:, p * LANES : (p + 1) * LANES]

    def gather(j):
        sem = ag_recv_sem.at[j]
        for d in range(1, Z):
            part = basis.at[j, c, :, yrows(y), lanes(x, z)]
            send(part, part, send_sem.at[1], sem.at[0], at_z(d))
        got = basis.at[j, c, :, pl.ds(0, ROWS), pl.ds(0, (Z - 1) * LANES)]
        wait_for(got, sem.at[0])
        wait_for(got, send_sem.at[1])

        a2 = basis.at[j, c, 0, yrows(y), xlanes(x)]
        b2 = basis.at[j, c, 1, yrows(y), xlanes(x)]
        for d in range(1, Y):
            send(a2, a2, send_sem.at[1], sem.at[1], at_y(d))
        for d in range(1, X):
            send(b2, b2, send_sem.at[2], sem.at[2], at_x(d))
        got = basis.at[j, c, 0, pl.ds(0, (Y - 1) * ROWS), pl.ds(0, span)]
        wait_for(got, sem.at[1])
        a3 = basis.at[j, c, 0, :, xlanes(x)]
        for d in range(1, X):
            send(a3, a3, send_sem.at[3], sem.at[2 + d], at_x(d))
        got = basis.at[j, c, 0, pl.ds(0, ROWS), pl.ds(0, (X - 1) * span)]
        wait_for(got, sem.at[2])
        b3 = basis.at[j, c, 1, yrows(y), :]
        for d in range(1, Y):
            send(b3, b3, send_sem.at[4], sem.at[1 + X + d], at_y(d))
        core = ag_core_sem.at[j]
        send(a3, a3, send_sem.at[5], core.at[0], sibling)
        send(b3, b3, send_sem.at[5], core.at[0], sibling)
        order = [1] + [d for d in range(3, max(X, Y))] + [2]
        for d in order:
            if d < X:
                a = basis.at[j, c, 0, :, xlanes(lax.rem(x - d + X, X))]
                wait_for(a, sem.at[2 + d])
                send(a, a, send_sem.at[5], core.at[0], sibling)
            if d < Y:
                b = basis.at[j, c, 1, yrows(lax.rem(y - d + Y, Y)), :]
                wait_for(b, sem.at[1 + X + d])
                send(b, b, send_sem.at[5], core.at[0], sibling)

    def gather_sent(j):
        wait_for(basis.at[j, c, 0, pl.ds(0, (Y - 1) * ROWS), pl.ds(0, span)], send_sem.at[1])
        wait_for(basis.at[j, c, 0, pl.ds(0, ROWS), pl.ds(0, (X - 1) * span)], send_sem.at[2])
        wait_for(basis.at[j, c, 0, :, pl.ds(0, (X - 1) * span)], send_sem.at[3])
        wait_for(basis.at[j, c, 1, pl.ds(0, (Y - 1) * ROWS), :], send_sem.at[4])
        wait_for(basis.at[j, c], send_sem.at[5])

    def contract(j, with_data):
        def half(cq, total):
            def body(zq, total):
                q, g = total
                for xq in range(X):
                    at = lanes(xq, zq)
                    left = jnp.concatenate([basis[j, cq, 0, :, at], basis[j, cq, 1, :, at]], axis=1)
                    if with_data:
                        q = q + nt(left, data_v[:, columns(xq, zq, cq)])
                    others = [
                        jnp.concatenate([basis[b, cq, 0, :, at], basis[b, cq, 1, :, at]], axis=1)
                        for b in range(j)
                    ] + [left]
                    g = g + nt(left, jnp.concatenate(others, axis=0) if j else left)
                return q, g

            return lax.fori_loop(0, Z, body, total)

        q = jnp.zeros((count, depth if with_data else LANES), F32)
        g = jnp.zeros((count, count * (j + 1)), F32)
        total = half(c, (q, g))
        wait_for(basis.at[j, o], ag_core_sem.at[j, 0])
        q, g = half(o, total)
        return q, [g[:, b * count : (b + 1) * count] for b in range(j + 1)]

    def reduce(k, pt):
        def piece(cq, xq, store):
            def body(zq, carry):
                r = jnp.dot(pt, data_v[:, columns(xq, zq, cq)], preferred_element_type=F32)
                store(zq, r)
                return carry

            lax.fori_loop(0, Z, body, 0, unroll=min(Z, 4))

        def compute(i):
            xq = lax.rem(x + 1 + i, X)

            def to_sibling(zq, r):
                for p in range(2):
                    pair_send[i, p, :, zlanes(zq)] = r[:, p * LANES : (p + 1) * LANES].astype(BF16)

            piece(o, xq, to_sibling)
            send(pair_send.at[i], pair_recv.at[i], send_sem.at[1], rs_core_sem.at[k, i], sibling)

            def keep(zq, r):
                for p in range(2):
                    own[i, p, :, zlanes(zq)] = r[:, p * LANES : (p + 1) * LANES]

            piece(c, xq, keep)

        def spread(i):
            xq = lax.rem(x + 1 + i, X)
            wait_for(pair_recv.at[i], rs_core_sem.at[k, i])
            both = own[i] + pair_recv[i].astype(F32)
            own[i] = both
            s1_send[i] = both.astype(BF16)
            if i < X - 1:
                d = i + 1
                send(
                    s1_send.at[i, 0], s1a_recv.at[d - 1], send_sem.at[2], rs1a_sem.at[k, d - 1], at_x(d)
                )
            for d in range(1, Y):
                send(
                    s1_send.at[i, 1, yrows(lax.rem(y + d, Y)), :],
                    s1b_recv.at[i, d - 1],
                    send_sem.at[3],
                    rs1b_sem.at[k, i],
                    at_y(d),
                )

        for i in range(X):
            compute(i)
            if i:
                spread(i - 1)
        spread(X - 1)

        for d in range(1, X):
            wait_for(s1a_recv.at[d - 1], rs1a_sem.at[k, d - 1])
        total = own[X - 1, 0]
        for d in range(1, X):
            total = total + s1a_recv[d - 1].astype(F32)
        own[X - 1, 0] = total
        s2_send[0] = total.astype(BF16)
        for d in range(1, Y):
            send(
                s2_send.at[0, yrows(lax.rem(y + d, Y)), :],
                s2_recv.at[0, d - 1],
                send_sem.at[4],
                rs2_sem.at[k, 0],
                at_y(d),
            )
        for i in range(X):
            wait_for(s1b_recv.at[i], rs1b_sem.at[k, i])
            total = own[i, 1, yrows(y), :]
            for d in range(1, Y):
                total = total + s1b_recv[i, d - 1].astype(F32)
            if i < X - 1:
                s2_send[1, pl.ds(i * ROWS, ROWS), :] = total.astype(BF16)
                send(
                    s2_send.at[1, pl.ds(i * ROWS, ROWS), :],
                    s2_recv.at[1, i],
                    send_sem.at[5],
                    rs2_sem.at[k, 1],
                    at_x(i + 1),
                )
        mine_b = total

        wait_for(s2_recv.at[0], rs2_sem.at[k, 0])
        total = own[X - 1, 0, yrows(y), :]
        for d in range(1, Y):
            total = total + s2_recv[0, d - 1].astype(F32)
        own[0, 0, pl.ds(0, ROWS), :] = total
        s3_send[0] = total.astype(BF16)
        wait_for(s2_recv.at[1], rs2_sem.at[k, 1])
        total = mine_b
        for d in range(1, X):
            total = total + s2_recv[1, d - 1].astype(F32)
        own[0, 1, pl.ds(0, ROWS), :] = total
        s3_send[1] = total.astype(BF16)
        for d in range(1, Z):
            send(
                s3_send.at[:, :, zlanes(lax.rem(z + d, Z))],
                s3_recv.at[d - 1],
                send_sem.at[6],
                rs3_sem.at[k],
                at_z(d),
            )
        wait_for(s3_recv, rs3_sem.at[k])
        total = own[0, :, pl.ds(0, ROWS), zlanes(z)]
        for d in range(1, Z):
            total = total + s3_recv[d - 1].astype(F32)
        basis[k + 1, c, :, yrows(y), lanes(x, z)] = total.astype(BF16)

        wait_for(pair_send, send_sem.at[1])
        wait_for(s1a_recv, send_sem.at[2])
        wait_for(s1b_recv, send_sem.at[3])
        wait_for(s2_recv.at[0], send_sem.at[4])
        wait_for(s2_recv.at[1], send_sem.at[5])
        wait_for(s3_recv, send_sem.at[6])

    row = lax.broadcasted_iota(jnp.int32, (count, count), 0)
    col = lax.broadcasted_iota(jnp.int32, (count, count), 1)
    eye = jnp.where(row == col, F32(1.0), F32(0.0))

    gather(0)
    load.wait()
    proj, (gvv,) = contract(0, True)
    coef = [eye]
    gather_sent(0)

    for k in range(STEPS):
        reduce(k, (proj.astype(BF16).astype(F32) * F32(1.0 / nrows)).astype(BF16))
        gather(k + 1)
        q, inner = contract(k + 1, k + 1 < STEPS)
        gram = exact(inner[0], coef[0], ((1,), (1,)))
        for b in range(1, k + 1):
            gram = gram + exact(inner[b], coef[b], ((1,), (1,)))
        weights = jnp.where(col < row, gram, F32(0.0))
        align = jnp.sum(eye * gram - weights * gvv, axis=1, keepdims=True)
        mix = eye * (F32(1.0) - F32(step_size) * align) - F32(step_size) * weights
        mixed = exact(mix, gvv)
        length = jnp.sum(
            mixed * mix + F32(2 * step_size) * mix * gram + F32(step_size**2) * eye * inner[k + 1],
            axis=1,
            keepdims=True,
        )
        scale = lax.rsqrt(length + F32(epsilon))
        if k + 1 < STEPS:
            proj = scale * (exact(mix, proj) + F32(step_size) * q)
            cross = exact(mix, gram, ((1,), (1,)))
            guu = (
                exact(mixed, mix, ((1,), (1,)))
                + F32(step_size) * (cross + cross.T)
                + F32(step_size**2) * inner[k + 1]
            )
            gvv = scale * guu * jnp.sum(eye * scale, axis=0, keepdims=True)
        coef = [scale * exact(mix, a) for a in coef] + [scale * F32(step_size) * eye]
        gather_sent(k + 1)

    at = lanes(x, z)
    total = jnp.zeros((count, 4 * LANES), F32)
    for b in range(STEPS + 1):
        wide_rows = jnp.concatenate(
            [basis[b, cq, p, :, at] for cq in range(2) for p in range(2)], axis=1
        ).astype(F32)
        total = total + exact(coef[b], wide_rows)
    rows_v[...] = total
    features = X * Z * 4 * LANES
    out_ref[...] = rows_v[pl.ds(pl.multiple_of(narrow * (ROWS // 2), ROWS // 2), ROWS // 2), :] * F32(
        features**0.5
    )


def on_device(data, players):
    Z = lax.axis_size("wide") // X
    depth, features = data.shape
    nrows = depth * lax.axis_size("wide") * lax.axis_size("narrow")
    count = Y * ROWS
    span = Z * LANES
    dma = pltpu.SemaphoreType.DMA
    flops = STEPS * 4 * count * features * depth
    return pl.pallas_call(
        functools.partial(kernel, Z, nrows),
        out_shape=jax.ShapeDtypeStruct(players.shape, F32),
        in_specs=[pl.BlockSpec(memory_space=pl.ANY), pl.BlockSpec(memory_space=pltpu.VMEM)],
        out_specs=pl.BlockSpec(memory_space=pltpu.VMEM),
        scratch_shapes=[
            pltpu.VMEM((depth, features), BF16),
            pltpu.VMEM((STEPS + 1, 2, 2, count, X * span), BF16),
            pltpu.VMEM((X, 2, count, span), BF16),
            pltpu.VMEM((X, 2, count, span), BF16),
            pltpu.VMEM((X, 2, count, span), F32),
            pltpu.VMEM((X, 2, count, span), BF16),
            pltpu.VMEM((X - 1, count, span), BF16),
            pltpu.VMEM((X, Y - 1, ROWS, span), BF16),
            pltpu.VMEM((2, count, span), BF16),
            pltpu.VMEM((2, max(X, Y) - 1, ROWS, span), BF16),
            pltpu.VMEM((2, ROWS, span), BF16),
            pltpu.VMEM((Z - 1, 2, ROWS, LANES), BF16),
            pltpu.VMEM((ROWS // 2, 2 * LANES), F32),
            pltpu.VMEM((count, 4 * LANES), F32),
            dma,
            dma((7,)),
            dma,
            dma((STEPS + 1, 1 + X + Y)),
            dma((STEPS + 1, 1)),
            dma((STEPS, X)),
            dma((STEPS, X - 1)),
            dma((STEPS, X)),
            dma((STEPS, 2)),
            dma((STEPS,)),
        ],
        compiler_params=pltpu.CompilerParams(
            collective_id=0, has_side_effects=True, vmem_limit_bytes=52 * 2**20
        ),
        cost_estimate=pl.CostEstimate(flops=flops, bytes_accessed=2 * depth * features, transcendentals=0),
    )(data, players)


def solution(mesh):
    placed = (P(("wide", "narrow"), None), P("narrow", "wide"))
    return jax.shard_map(
        on_device, mesh=mesh, in_specs=placed, out_specs=P("narrow", "wide"), check_vma=False
    )
```

time: 1730 us -> 164 us (0.09)
  the two profiles are of different devices: /device:TPU:8 before, /device:TPU:1 now
where the time goes in v1:
time: 164 us; the launch traced here: 163 us
  Pallas kernels  162 us (99%)
    pallas_call x1, Pallas kernels, on_device(): pl.pallas_call(functools.partial(kernel, Z, nrows), out_shape=jax.ShapeDt...  162 us

profile of v1, /device:TPU:1, one launch (start us, length us, event | category | flops | bytes accessed | tf_op | source)
XLA Modules:
  0.0 163.4 jit_solution(16782837628428077878)
XLA Ops:
  0.0 0.0 copy-start
  0.0 0.7 copy-done
  0.7 162.1 %shard_map.28 = f32[8,512]{1,0:T(8,128)S(1)} custom-call(bf16[256,16384]{1,0:T(8,128)(2,1)} %data_hbm.1, f32[8,512]{1,0:T(8,128)S(1)} %copy-done), custom_call_target="tpu_custom_call" | custom-call | flops 3221225472 | bytes 8388608 | tf_op jit(solution)/shard_map/pallas_call | solution.py:387
  162.8 0.6 copy.4
Async XLA Ops:
  0.0 0.7 copy-start

commit v2 on v0

v2 whole, which is shorter than its diff:
```python
import functools

import jax
import jax.numpy as jnp
from jax import lax
from jax.experimental import pallas as pl
from jax.experimental.pallas import tpu as pltpu
from jax.sharding import PartitionSpec as P

STEPS = 3
step_size = 0.5
epsilon = 1e-06

X = 4
Y = 4
ROWS = 16
HALF = ROWS // 2
LANES = 256
UNITS = 4

MESH = pl.DeviceIdType.MESH
F32 = jnp.float32
BF16 = jnp.bfloat16


def exact(a, b, contract=((1,), (0,))):
    return lax.dot_general(
        a, b, (contract, ((), ())), precision=lax.Precision.HIGHEST, preferred_element_type=F32
    )


def nt(a, b):
    return lax.dot_general(a, b, (((1,), (1,)), ((), ())), preferred_element_type=F32)


def kernel(
    Z,
    nrows,
    data_hbm,
    players_ref,
    out_ref,
    data_v,
    basis,
    players_recv,
    part_send,
    part_recv,
    s1_send,
    s1_recv,
    s2_send,
    s2_recv,
    s2_own,
    s3_send,
    z_recv,
    last_recv,
    gram_send,
    gram_recv,
    gram_z_recv,
    sq_send,
    sq_recv,
    sq_z_recv,
    sq_core_recv,
    upd_v,
    upd_recv,
    gvv_v,
    load_sem,
    swap_send_sem,
    swap_recv_sem,
    send_sem,
    first_sem,
    part_sem,
    z0_sem,
    s1_sem,
    s2_sem,
    s3_sem,
    s4_sem,
    s5_sem,
    gram_sem,
    sq_sem,
    upd_sem,
):
    U = min(UNITS, Z)
    zpu = Z // U
    wide = lax.axis_index("wide")
    narrow = lax.axis_index("narrow")
    z, x = wide // X, wide % X
    y, c = narrow // 2, narrow % 2
    o = 1 - c
    count = Y * ROWS
    span = zpu * LANES
    unit = X * span
    depth = data_hbm.shape[0]

    def at_x(d):
        return (z * X + lax.rem(x + d, X), narrow)

    def at_y(d):
        return (wide, lax.rem(y + d, Y) * 2 + c)

    def at_z(d):
        return (lax.rem(z + d, Z) * X + x, narrow)

    sibling = (wide, y * 2 + o)

    def piece(at, size):
        return pl.ds(pl.multiple_of(at * size, size), size)

    def send(src, dst, ssem, rsem, where):
        pltpu.make_async_remote_copy(
            src_ref=src, dst_ref=dst, send_sem=ssem, recv_sem=rsem, device_id=where, device_id_type=MESH
        ).start()

    def wait_for(ref, sem):
        pltpu.make_async_copy(ref, ref, sem).wait()

    barrier = pltpu.get_barrier_semaphore()
    peers = [sibling]
    peers += [at_x(d) for d in range(1, X)]
    peers += [at_y(d) for d in range(1, Y)]
    peers += [at_z(d) for d in range(1, Z)]
    for peer in peers:
        pl.semaphore_signal(barrier, inc=1, device_id=peer, device_id_type=MESH)
    pl.semaphore_wait(barrier, len(peers))

    send(players_ref.at[:, piece(o, LANES)], players_recv, send_sem.at[0], first_sem, sibling)

    def swap(q, carry):
        zq, xq = q // X, lax.rem(q, X)
        to = piece(((zq // zpu) * X + xq) * zpu + lax.rem(zq, zpu), LANES)
        rows = piece(c, depth)
        pltpu.make_async_copy(data_hbm.at[:, piece(q * 2 + c, LANES)], data_v.at[rows, to], load_sem).start()
        send(
            data_hbm.at[:, piece(q * 2 + o, LANES)], data_v.at[rows, to], swap_send_sem, swap_recv_sem, sibling
        )
        return carry

    lax.fori_loop(0, Z * X, swap, 0)

    wait_for(players_recv, first_sem)
    mine = players_ref[:, piece(c, LANES)]
    theirs = players_recv[...]
    my_block = (z // zpu, pl.ds(pl.multiple_of(y * ROWS, ROWS), ROWS), piece(x * zpu + lax.rem(z, zpu), LANES))
    basis[(0, *my_block)] = jnp.where(
        c == 0, jnp.concatenate([mine, theirs], axis=0), jnp.concatenate([theirs, mine], axis=0)
    ).astype(BF16)
    for d in range(1, Z):
        part = basis.at[(0, *my_block)]
        send(part, part, send_sem.at[1], z0_sem, at_z(d))

    def fourth(j, u):
        part = basis.at[j, u, piece(y, ROWS), piece(x, span)]
        if u % 2 == 0:
            for d in range(1, Y):
                send(part, part, send_sem.at[2], s4_sem.at[j, u], at_y(d))
        else:
            for d in range(1, X):
                send(part, part, send_sem.at[2], s4_sem.at[j, u], at_x(d))

    def fifth(j, u):
        if u % 2 == 0:
            wait_for(s2_recv.at[u, pl.ds(0, Y - 1)], s4_sem.at[j, u])
            part = basis.at[j, u, :, piece(x, span)]
            for d in range(1, X):
                send(part, part, send_sem.at[3], s5_sem.at[j, u], at_x(d))
        else:
            wait_for(s2_recv.at[u, pl.ds(0, X - 1)], s4_sem.at[j, u])
            part = basis.at[j, u, piece(y, ROWS), :]
            for d in range(1, Y):
                send(part, part, send_sem.at[3], s5_sem.at[j, u], at_y(d))

    def contract(j, u):
        if u % 2 == 0:
            wait_for(basis.at[j, u, :, pl.ds(0, (X - 1) * span)], s5_sem.at[j, u])
        else:
            wait_for(basis.at[j, u, pl.ds(0, (Y - 1) * ROWS), :], s5_sem.at[j, u])
        if j == 0 and u == 0:
            wait_for(data_v.at[pl.ds(0, depth)], load_sem)
            wait_for(data_v.at[pl.ds(0, depth)], swap_recv_sem)
        left = basis[j, u]
        q = nt(left, data_v[:, u * unit : (u + 1) * unit])
        g = jnp.concatenate([nt(left, basis[b, u]) for b in range(j + 1)], axis=1)
        if u == 0:
            part_send[j, :, : 2 * depth] = q
            part_send[j, :, 2 * depth : 2 * depth + (j + 1) * count] = g
        else:
            part_send[j, :, : 2 * depth] += q
            part_send[j, :, 2 * depth : 2 * depth + (j + 1) * count] += g

    def whole(j):
        part = part_send.at[j]
        send(part, part_recv.at[j], send_sem.at[4], part_sem.at[j], sibling)
        wait_for(part, part_sem.at[j])
        total = part_send[j, :, : 2 * depth + (j + 1) * count] + part_recv[j, :, : 2 * depth + (j + 1) * count]
        return total[:, : 2 * depth], [
            total[:, 2 * depth + b * count : 2 * depth + (b + 1) * count] for b in range(j + 1)
        ]

    def gather_sent(j):
        for u in range(U):
            peers4, peers5 = (Y - 1, X - 1) if u % 2 == 0 else (X - 1, Y - 1)
            wait_for(s2_recv.at[u, pl.ds(0, peers4)], send_sem.at[2])
            if u % 2 == 0:
                wait_for(basis.at[j, u, :, pl.ds(0, (X - 1) * span)], send_sem.at[3])
            else:
                wait_for(basis.at[j, u, pl.ds(0, (Y - 1) * ROWS), :], send_sem.at[3])
        wait_for(part_send.at[j], send_sem.at[4])

    def first_stage(k, u, pt):
        for xq in range(X):
            at = u * unit + xq * span
            r = jnp.dot(pt, data_v[:, at : at + span], preferred_element_type=F32)
            s1_send[u, :, xq * span : (xq + 1) * span] = r.astype(BF16)
        if u % 2 == 0:
            for d in range(1, X):
                send(
                    s1_send.at[u, :, piece(lax.rem(x + d, X), span)],
                    s1_recv.at[u, :, pl.ds((d - 1) * span, span)],
                    send_sem.at[5],
                    s1_sem.at[k, u],
                    at_x(d),
                )
        else:
            for d in range(1, Y):
                send(
                    s1_send.at[u, piece(lax.rem(y + d, Y), ROWS), :],
                    s1_recv.at[u, pl.ds((d - 1) * ROWS, ROWS), :],
                    send_sem.at[5],
                    s1_sem.at[k, u],
                    at_y(d),
                )

    def second_stage(k, u):
        if u % 2 == 0:
            wait_for(s1_recv.at[u, :, pl.ds(0, (X - 1) * span)], s1_sem.at[k, u])
            total = s1_send[u, :, piece(x, span)].astype(F32)
            for d in range(1, X):
                total = total + s1_recv[u, :, (d - 1) * span : d * span].astype(F32)
            s2_send[u] = total.astype(BF16)
            for d in range(1, Y):
                send(
                    s2_send.at[u, piece(lax.rem(y + d, Y), ROWS), :],
                    s2_recv.at[u, d - 1],
                    send_sem.at[6],
                    s2_sem.at[k, u],
                    at_y(d),
                )
        else:
            wait_for(s1_recv.at[u, pl.ds(0, (Y - 1) * ROWS), :], s1_sem.at[k, u])
            total = s1_send[u, piece(y, ROWS), :].astype(F32)
            for d in range(1, Y):
                total = total + s1_recv[u, (d - 1) * ROWS : d * ROWS, :].astype(F32)
            for xq in range(X):
                s2_send[u, xq * ROWS : (xq + 1) * ROWS, :] = total[:, xq * span : (xq + 1) * span].astype(BF16)
            for d in range(1, X):
                send(
                    s2_send.at[u, piece(lax.rem(x + d, X), ROWS), :],
                    s2_recv.at[u, d - 1],
                    send_sem.at[6],
                    s2_sem.at[k, u],
                    at_x(d),
                )

    def plane_sum(k, u):
        n = Y if u % 2 == 0 else X
        wait_for(s2_recv.at[u, pl.ds(0, n - 1)], s2_sem.at[k, u])
        total = s2_send[u, piece(y if u % 2 == 0 else x, ROWS), :].astype(F32)
        for d in range(1, n):
            total = total + s2_recv[u, d - 1].astype(F32)
        return total

    def third_stage(k, u):
        total = plane_sum(k, u)
        s2_own[u] = total
        s3_send[u] = total.astype(BF16)
        for d in range(1, Z):
            send(s3_send.at[u], z_recv.at[k, u, d - 1], send_sem.at[7], s3_sem.at[k, u], at_z(d))

    def rows_done(k, u):
        wait_for(z_recv.at[k, u], s3_sem.at[k, u])
        total = s2_own[u]
        for d in range(1, Z):
            total = total + z_recv[k, u, d - 1].astype(F32)
        basis[k + 1, u, piece(y, ROWS), piece(x, span)] = total.astype(BF16)
        fourth(k + 1, u)

    def reduce_sent(k):
        for u in range(U):
            if u % 2 == 0:
                wait_for(s1_recv.at[u, :, pl.ds(0, (X - 1) * span)], send_sem.at[5])
                wait_for(s2_recv.at[u, pl.ds(0, Y - 1)], send_sem.at[6])
            else:
                wait_for(s1_recv.at[u, pl.ds(0, (Y - 1) * ROWS), :], send_sem.at[5])
                wait_for(s2_recv.at[u, pl.ds(0, X - 1)], send_sem.at[6])

    row = lax.broadcasted_iota(jnp.int32, (count, count), 0)
    col = lax.broadcasted_iota(jnp.int32, (count, count), 1)
    eye = jnp.where(row == col, F32(1.0), F32(0.0))

    def weigh(gram, gvv, lower, diagonal):
        weights = jnp.where(lower, gram, F32(0.0))
        align = jnp.sum(diagonal * gram - weights * gvv, axis=1, keepdims=True)
        return diagonal * (F32(1.0) - F32(step_size) * align) - F32(step_size) * weights

    wait_for(z_recv.at[0, 0, :, :, pl.ds(0, LANES)], z0_sem)
    for u in range(U):
        fourth(0, u)
    for u in range(U):
        fifth(0, u)
    for u in range(U):
        contract(0, u)
    proj, (gvv,) = whole(0)
    coef = [eye]
    wait_for(players_recv, send_sem.at[0])
    wait_for(z_recv.at[0, 0, :, :, pl.ds(0, LANES)], send_sem.at[1])
    wait_for(data_v.at[pl.ds(0, depth)], swap_send_sem)

    for k in range(STEPS - 1):
        pt = (proj.astype(BF16).astype(F32) * F32(1.0 / nrows)).astype(BF16)
        for u in range(U):
            first_stage(k, u, pt)
        gather_sent(k)
        for u in range(U):
            second_stage(k, u)
        for u in range(U):
            third_stage(k, u)
        for u in range(U):
            rows_done(k, u)
        for u in range(U):
            fifth(k + 1, u)
        for u in range(U):
            contract(k + 1, u)
        q, inner = whole(k + 1)
        gram = exact(inner[0], coef[0], ((1,), (1,)))
        for b in range(1, k + 1):
            gram = gram + exact(inner[b], coef[b], ((1,), (1,)))
        mix = weigh(gram, gvv, col < row, eye)
        mixed = exact(mix, gvv)
        length = jnp.sum(
            mixed * mix + F32(2 * step_size) * mix * gram + F32(step_size**2) * eye * inner[k + 1],
            axis=1,
            keepdims=True,
        )
        scale = lax.rsqrt(length + F32(epsilon))
        proj = scale * (exact(mix, proj) + F32(step_size) * q)
        cross = exact(mix, gram, ((1,), (1,)))
        guu = (
            exact(mixed, mix, ((1,), (1,)))
            + F32(step_size) * (cross + cross.T)
            + F32(step_size**2) * inner[k + 1]
        )
        gvv = scale * guu * jnp.sum(eye * scale, axis=0, keepdims=True)
        coef = [scale * exact(mix, a) for a in coef] + [scale * F32(step_size) * eye]
        reduce_sent(k)
        wait_for(z_recv.at[k], send_sem.at[7])

    k = STEPS - 1
    pt = (proj.astype(BF16).astype(F32) * F32(1.0 / nrows)).astype(BF16)
    gram = exact(pt.astype(F32), proj, ((1,), (1,)))
    gram_send[0] = jnp.concatenate([gram, jnp.zeros((count, 128 - count), F32)], axis=1)
    for d in range(1, Y):
        send(
            gram_send.at[0, piece(lax.rem(y + d, Y), ROWS), :],
            gram_recv.at[0, d - 1],
            send_sem.at[8],
            gram_sem.at[0],
            at_y(d),
        )
    for u in range(U):
        first_stage(k, u, pt)
    gather_sent(k)
    wait_for(gram_recv.at[0, pl.ds(0, Y - 1)], gram_sem.at[0])
    total = gram_send[0, piece(y, ROWS), :]
    for d in range(1, Y):
        total = total + gram_recv[0, d - 1]
    gram_send[1, :ROWS, :] = total
    for d in range(1, X):
        send(
            gram_send.at[1, pl.ds(0, ROWS)], gram_recv.at[1, d - 1], send_sem.at[9], gram_sem.at[1], at_x(d)
        )
    for u in range(U):
        second_stage(k, u)
    wait_for(gram_recv.at[1, pl.ds(0, X - 1)], gram_sem.at[1])
    total = gram_send[1, :ROWS, :]
    for d in range(1, X):
        total = total + gram_recv[1, d - 1]
    gram_send[2, :ROWS, :] = total
    for d in range(1, Z):
        send(
            gram_send.at[2, pl.ds(0, ROWS)], gram_z_recv.at[d - 1], send_sem.at[10], gram_sem.at[2], at_z(d)
        )
    for u in range(U):
        total = plane_sum(k, u)
        s2_own[u] = total
        s3_send[u] = total.astype(BF16)
    for d in range(1, Z):
        zq = lax.rem(z + d, Z)
        send(
            s3_send.at[zq // zpu, :, piece(lax.rem(zq, zpu), LANES)],
            last_recv.at[d - 1],
            send_sem.at[7],
            s3_sem.at[k, 0],
            at_z(d),
        )
    v = jnp.zeros((count, LANES), F32)
    for b in range(STEPS):
        v = v + exact(coef[b], basis[b, z // zpu, :, piece(x * zpu + lax.rem(z, zpu), LANES)].astype(F32))
    gvv_v[...] = gvv
    row = lax.broadcasted_iota(jnp.int32, (ROWS, count), 0) + y * ROWS
    col = lax.broadcasted_iota(jnp.int32, (ROWS, count), 1)
    wait_for(gram_z_recv, gram_sem.at[2])
    total = gram_send[2, :ROWS, :]
    for d in range(1, Z):
        total = total + gram_z_recv[d - 1]
    mix = weigh(
        total[:, :count], gvv_v[piece(y, ROWS), :], col < row, jnp.where(row == col, F32(1.0), F32(0.0))
    )
    upd = exact(mix, v)
    wait_for(last_recv, s3_sem.at[k, 0])
    moved = s2_own[z // zpu, :, piece(lax.rem(z, zpu), LANES)]
    for d in range(1, Z):
        moved = moved + last_recv[d - 1].astype(F32)
    upd = upd + F32(step_size) * moved
    upd_v[...] = upd
    send(upd_v.at[piece(o, HALF), :], upd_recv, send_sem.at[0], upd_sem, sibling)
    sq_send[0] = jnp.broadcast_to(jnp.sum(upd * upd, axis=1, keepdims=True), (ROWS, 128))
    for d in range(1, Z):
        send(sq_send.at[0], sq_z_recv.at[d - 1], send_sem.at[1], sq_sem.at[0], at_z(d))
    wait_for(sq_z_recv, sq_sem.at[0])
    total = sq_send[0]
    for d in range(1, Z):
        total = total + sq_z_recv[d - 1]
    sq_send[1] = total
    for d in range(1, X):
        send(sq_send.at[1], sq_recv.at[d - 1], send_sem.at[2], sq_sem.at[1], at_x(d))
    wait_for(sq_recv, sq_sem.at[1])
    total = sq_send[1]
    for d in range(1, X):
        total = total + sq_recv[d - 1]
    sq_send[2] = total
    send(sq_send.at[2], sq_core_recv, send_sem.at[3], sq_sem.at[2], sibling)
    wait_for(sq_core_recv, sq_sem.at[2])
    wait_for(upd_recv, upd_sem)
    length = (sq_send[2, piece(c, HALF), :] + sq_core_recv[piece(c, HALF), :])[:, :1]
    scale = lax.rsqrt(length + F32(epsilon)) * F32((Z * X * 2 * LANES) ** 0.5)
    out_ref[:, piece(c, LANES)] = upd_v[piece(c, HALF), :] * scale
    out_ref[:, piece(o, LANES)] = upd_recv[...] * scale

    reduce_sent(k)
    wait_for(last_recv, send_sem.at[7])
    wait_for(gram_recv.at[0, pl.ds(0, Y - 1)], send_sem.at[8])
    wait_for(gram_recv.at[1, pl.ds(0, X - 1)], send_sem.at[9])
    wait_for(gram_z_recv, send_sem.at[10])
    wait_for(upd_recv, send_sem.at[0])
    wait_for(sq_z_recv, send_sem.at[1])
    wait_for(sq_recv, send_sem.at[2])
    wait_for(sq_core_recv, send_sem.at[3])


def on_device(data, players):
    Z = lax.axis_size("wide") // X
    U = min(UNITS, Z)
    depth, features = data.shape
    nrows = depth * lax.axis_size("wide") * lax.axis_size("narrow")
    count = Y * ROWS
    span = Z // U * LANES
    most = max(X, Y) - 1
    parts = 2 * depth + STEPS * count
    parts = -(-parts // 128) * 128
    dma = pltpu.SemaphoreType.DMA
    flops = STEPS * 4 * count * features * depth
    return pl.pallas_call(
        functools.partial(kernel, Z, nrows),
        out_shape=jax.ShapeDtypeStruct(players.shape, F32),
        in_specs=[pl.BlockSpec(memory_space=pl.ANY), pl.BlockSpec(memory_space=pltpu.VMEM)],
        out_specs=pl.BlockSpec(memory_space=pltpu.VMEM),
        scratch_shapes=[
            pltpu.VMEM((2 * depth, features // 2), BF16),
            pltpu.VMEM((STEPS, U, count, X * span), BF16),
            pltpu.VMEM((HALF, LANES), F32),
            pltpu.VMEM((STEPS, count, parts), F32),
            pltpu.VMEM((STEPS, count, parts), F32),
            pltpu.VMEM((U, count, X * span), BF16),
            pltpu.VMEM((U, count, X * span), BF16),
            pltpu.VMEM((U, max(X, Y) * ROWS, span), BF16),
            pltpu.VMEM((U, most, ROWS, span), BF16),
            pltpu.VMEM((U, ROWS, span), F32),
            pltpu.VMEM((U, ROWS, span), BF16),
            pltpu.VMEM((STEPS - 1, U, Z - 1, ROWS, span), BF16),
            pltpu.VMEM((Z - 1, ROWS, LANES), BF16),
            pltpu.VMEM((3, count, 128), F32),
            pltpu.VMEM((2, most, ROWS, 128), F32),
            pltpu.VMEM((Z - 1, ROWS, 128), F32),
            pltpu.VMEM((3, ROWS, 128), F32),
            pltpu.VMEM((X - 1, ROWS, 128), F32),
            pltpu.VMEM((Z - 1, ROWS, 128), F32),
            pltpu.VMEM((ROWS, 128), F32),
            pltpu.VMEM((ROWS, LANES), F32),
            pltpu.VMEM((HALF, LANES), F32),
            pltpu.VMEM((count, count), F32),
            dma,
            dma,
            dma,
            dma((11,)),
            dma,
            dma((STEPS,)),
            dma,
            dma((STEPS, U)),
            dma((STEPS, U)),
            dma((STEPS, U)),
            dma((STEPS, U)),
            dma((STEPS, U)),
            dma((3,)),
            dma((3,)),
            dma,
        ],
        compiler_params=pltpu.CompilerParams(
            collective_id=0, has_side_effects=True, vmem_limit_bytes=52 * 2**20
        ),
        cost_estimate=pl.CostEstimate(flops=flops, bytes_accessed=2 * depth * features, transcendentals=0),
    )(data, players)


def solution(mesh):
    placed = (P(("wide", "narrow"), None), P("narrow", "wide"))
    return jax.shard_map(
        on_device, mesh=mesh, in_specs=placed, out_specs=P("narrow", "wide"), check_vma=False
    )
```

time: 1730 us -> 133 us (0.08)
  the two profiles are of different devices: /device:TPU:8 before, /device:TPU:1 now
where the time goes in v2:
time: 133 us
  Pallas kernels  132 us (99%)
    pallas_call x1, Pallas kernels, on_device(): pl.pallas_call(functools.partial(kernel, Z, nrows), out_shape=jax.ShapeDt...  132 us

profile of v2, /device:TPU:1, one launch (start us, length us, event | category | flops | bytes accessed | tf_op | source)
XLA Modules:
  0.0 133.1 jit_solution(445759310816109638)
XLA Ops:
  0.0 0.0 copy-start
  0.0 0.7 copy-done
  0.7 131.8 %shard_map.28 = f32[8,512]{1,0:T(8,128)S(1)} custom-call(bf16[256,16384]{1,0:T(8,128)(2,1)} %data_hbm.1, f32[8,512]{1,0:T(8,128)S(1)} %copy-done), custom_call_target="tpu_custom_call" | custom-call | flops 3221225472 | bytes 8388608 | tf_op jit(solution)/shard_map/pallas_call | solution.py:470
  132.5 0.6 copy.4
Async XLA Ops:
  0.0 0.7 copy-start

commit v3 on v2

--- a/solution.py
+++ b/solution.py
@@ -16,7 +16,6 @@
 ROWS = 16
 HALF = ROWS // 2
 LANES = 256
-UNITS = 4
 
 MESH = pl.DeviceIdType.MESH
 F32 = jnp.float32
@@ -51,7 +50,6 @@
     s2_own,
     s3_send,
     z_recv,
-    last_recv,
     gram_send,
     gram_recv,
     gram_z_recv,
@@ -68,7 +66,7 @@
     send_sem,
     first_sem,
     part_sem,
-    z0_sem,
+    za_sem,
     s1_sem,
     s2_sem,
     s3_sem,
@@ -78,16 +76,16 @@
     sq_sem,
     upd_sem,
 ):
-    U = min(UNITS, Z)
-    zpu = Z // U
     wide = lax.axis_index("wide")
     narrow = lax.axis_index("narrow")
     z, x = wide // X, wide % X
     y, c = narrow // 2, narrow % 2
     o = 1 - c
     count = Y * ROWS
-    span = zpu * LANES
+    span = LANES
     unit = X * span
+    near = sorted(range(Z), key=lambda d: (min(d, Z - d), d))
+    far = near[::-1]
     depth = data_hbm.shape[0]
 
     def at_x(d):
@@ -111,6 +109,15 @@
 
     def wait_for(ref, sem):
         pltpu.make_async_copy(ref, ref, sem).wait()
+
+    def place(q):
+        return piece(c, depth), piece(lax.rem(q // X - z + Z, Z) * X + lax.rem(q, X), LANES)
+
+    def load(q, carry):
+        pltpu.make_async_copy(data_hbm.at[:, piece(q * 2 + c, LANES)], data_v.at[place(q)], load_sem).start()
+        return carry
+
+    lax.fori_loop(0, Z * X, load, 0)
 
     barrier = pltpu.get_barrier_semaphore()
     peers = [sibling]
@@ -123,30 +130,36 @@
 
     send(players_ref.at[:, piece(o, LANES)], players_recv, send_sem.at[0], first_sem, sibling)
 
-    def swap(q, carry):
-        zq, xq = q // X, lax.rem(q, X)
-        to = piece(((zq // zpu) * X + xq) * zpu + lax.rem(zq, zpu), LANES)
-        rows = piece(c, depth)
-        pltpu.make_async_copy(data_hbm.at[:, piece(q * 2 + c, LANES)], data_v.at[rows, to], load_sem).start()
-        send(
-            data_hbm.at[:, piece(q * 2 + o, LANES)], data_v.at[rows, to], swap_send_sem, swap_recv_sem, sibling
-        )
-        return carry
-
-    lax.fori_loop(0, Z * X, swap, 0)
-
     wait_for(players_recv, first_sem)
     mine = players_ref[:, piece(c, LANES)]
     theirs = players_recv[...]
-    my_block = (z // zpu, pl.ds(pl.multiple_of(y * ROWS, ROWS), ROWS), piece(x * zpu + lax.rem(z, zpu), LANES))
-    basis[(0, *my_block)] = jnp.where(
+    basis[0, 0, piece(y, ROWS), piece(x, span)] = jnp.where(
         c == 0, jnp.concatenate([mine, theirs], axis=0), jnp.concatenate([theirs, mine], axis=0)
     ).astype(BF16)
-    for d in range(1, Z):
-        part = basis.at[(0, *my_block)]
-        send(part, part, send_sem.at[1], z0_sem, at_z(d))
+
+    def along_z(j):
+        for d in near[1:]:
+            send(
+                basis.at[j, 0, piece(y, ROWS), piece(x, span)],
+                basis.at[j, Z - d, piece(y, ROWS), piece(x, span)],
+                send_sem.at[1],
+                za_sem.at[j, Z - d],
+                at_z(d),
+            )
+
+    def swap(q, carry):
+        send(
+            data_hbm.at[:, piece(q * 2 + o, LANES)],
+            data_v.at[place(q)],
+            swap_send_sem,
+            swap_recv_sem,
+            sibling,
+        )
+        return carry
 
     def fourth(j, u):
+        if u:
+            wait_for(z_recv.at[0, 0], za_sem.at[j, u])
         part = basis.at[j, u, piece(y, ROWS), piece(x, span)]
         if u % 2 == 0:
             for d in range(1, Y):
@@ -172,13 +185,13 @@
             wait_for(basis.at[j, u, :, pl.ds(0, (X - 1) * span)], s5_sem.at[j, u])
         else:
             wait_for(basis.at[j, u, pl.ds(0, (Y - 1) * ROWS), :], s5_sem.at[j, u])
-        if j == 0 and u == 0:
+        if j == 0 and u == near[0]:
             wait_for(data_v.at[pl.ds(0, depth)], load_sem)
             wait_for(data_v.at[pl.ds(0, depth)], swap_recv_sem)
         left = basis[j, u]
         q = nt(left, data_v[:, u * unit : (u + 1) * unit])
         g = jnp.concatenate([nt(left, basis[b, u]) for b in range(j + 1)], axis=1)
-        if u == 0:
+        if u == near[0]:
             part_send[j, :, : 2 * depth] = q
             part_send[j, :, 2 * depth : 2 * depth + (j + 1) * count] = g
         else:
@@ -194,8 +207,21 @@
             total[:, 2 * depth + b * count : 2 * depth + (b + 1) * count] for b in range(j + 1)
         ]
 
+    def gather(j):
+        fourth(j, 0)
+        for u in near[1:3]:
+            fourth(j, u)
+        fifth(j, 0)
+        for u in near[3:]:
+            fourth(j, u)
+        for u in near[1:]:
+            fifth(j, u)
+        for u in near:
+            contract(j, u)
+
     def gather_sent(j):
-        for u in range(U):
+        wait_for(z_recv.at[0], send_sem.at[1])
+        for u in range(Z):
             peers4, peers5 = (Y - 1, X - 1) if u % 2 == 0 else (X - 1, Y - 1)
             wait_for(s2_recv.at[u, pl.ds(0, peers4)], send_sem.at[2])
             if u % 2 == 0:
@@ -269,21 +295,31 @@
 
     def third_stage(k, u):
         total = plane_sum(k, u)
-        s2_own[u] = total
-        s3_send[u] = total.astype(BF16)
+        if u:
+            s3_send[u - 1] = total.astype(BF16)
+            send(s3_send.at[u - 1], z_recv.at[k, u - 1], send_sem.at[7], s3_sem.at[k], at_z(u))
+        return total
+
+    def reduce(k, pt):
+        for u in far:
+            first_stage(k, u, pt)
+        gather_sent(k)
+        for u in far:
+            second_stage(k, u)
+        for u in far:
+            total = third_stage(k, u)
+        s2_own[...] = total
+
+    def rows_of_block(k):
+        wait_for(z_recv.at[k], s3_sem.at[k])
+        total = s2_own[...]
         for d in range(1, Z):
-            send(s3_send.at[u], z_recv.at[k, u, d - 1], send_sem.at[7], s3_sem.at[k, u], at_z(d))
-
-    def rows_done(k, u):
-        wait_for(z_recv.at[k, u], s3_sem.at[k, u])
-        total = s2_own[u]
-        for d in range(1, Z):
-            total = total + z_recv[k, u, d - 1].astype(F32)
-        basis[k + 1, u, piece(y, ROWS), piece(x, span)] = total.astype(BF16)
-        fourth(k + 1, u)
+            total = total + z_recv[k, d - 1].astype(F32)
+        return total
 
     def reduce_sent(k):
-        for u in range(U):
+        wait_for(z_recv.at[k], send_sem.at[7])
+        for u in range(Z):
             if u % 2 == 0:
                 wait_for(s1_recv.at[u, :, pl.ds(0, (X - 1) * span)], send_sem.at[5])
                 wait_for(s2_recv.at[u, pl.ds(0, Y - 1)], send_sem.at[6])
@@ -300,34 +336,20 @@
         align = jnp.sum(diagonal * gram - weights * gvv, axis=1, keepdims=True)
         return diagonal * (F32(1.0) - F32(step_size) * align) - F32(step_size) * weights
 
-    wait_for(z_recv.at[0, 0, :, :, pl.ds(0, LANES)], z0_sem)
-    for u in range(U):
-        fourth(0, u)
-    for u in range(U):
-        fifth(0, u)
-    for u in range(U):
-        contract(0, u)
+    along_z(0)
+    lax.fori_loop(0, Z * X, swap, 0)
+    gather(0)
     proj, (gvv,) = whole(0)
     coef = [eye]
     wait_for(players_recv, send_sem.at[0])
-    wait_for(z_recv.at[0, 0, :, :, pl.ds(0, LANES)], send_sem.at[1])
     wait_for(data_v.at[pl.ds(0, depth)], swap_send_sem)
 
     for k in range(STEPS - 1):
         pt = (proj.astype(BF16).astype(F32) * F32(1.0 / nrows)).astype(BF16)
-        for u in range(U):
-            first_stage(k, u, pt)
-        gather_sent(k)
-        for u in range(U):
-            second_stage(k, u)
-        for u in range(U):
-            third_stage(k, u)
-        for u in range(U):
-            rows_done(k, u)
-        for u in range(U):
-            fifth(k + 1, u)
-        for u in range(U):
-            contract(k + 1, u)
+        reduce(k, pt)
+        basis[k + 1, 0, piece(y, ROWS), piece(x, span)] = rows_of_block(k).astype(BF16)
+        along_z(k + 1)
+        gather(k + 1)
         q, inner = whole(k + 1)
         gram = exact(inner[0], coef[0], ((1,), (1,)))
         for b in range(1, k + 1):
@@ -350,7 +372,6 @@
         gvv = scale * guu * jnp.sum(eye * scale, axis=0, keepdims=True)
         coef = [scale * exact(mix, a) for a in coef] + [scale * F32(step_size) * eye]
         reduce_sent(k)
-        wait_for(z_recv.at[k], send_sem.at[7])
 
     k = STEPS - 1
     pt = (proj.astype(BF16).astype(F32) * F32(1.0 / nrows)).astype(BF16)
@@ -364,7 +385,7 @@
             gram_sem.at[0],
             at_y(d),
         )
-    for u in range(U):
+    for u in far:
         first_stage(k, u, pt)
     gather_sent(k)
     wait_for(gram_recv.at[0, pl.ds(0, Y - 1)], gram_sem.at[0])
@@ -376,7 +397,7 @@
         send(
             gram_send.at[1, pl.ds(0, ROWS)], gram_recv.at[1, d - 1], send_sem.at[9], gram_sem.at[1], at_x(d)
         )
-    for u in range(U):
+    for u in far:
         second_stage(k, u)
     wait_for(gram_recv.at[1, pl.ds(0, X - 1)], gram_sem.at[1])
     total = gram_send[1, :ROWS, :]
@@ -387,22 +408,12 @@
         send(
             gram_send.at[2, pl.ds(0, ROWS)], gram_z_recv.at[d - 1], send_sem.at[10], gram_sem.at[2], at_z(d)
         )
-    for u in range(U):
-        total = plane_sum(k, u)
-        s2_own[u] = total
-        s3_send[u] = total.astype(BF16)
-    for d in range(1, Z):
-        zq = lax.rem(z + d, Z)
-        send(
-            s3_send.at[zq // zpu, :, piece(lax.rem(zq, zpu), LANES)],
-            last_recv.at[d - 1],
-            send_sem.at[7],
-            s3_sem.at[k, 0],
-            at_z(d),
-        )
+    for u in far:
+        total = third_stage(k, u)
+    s2_own[...] = total
     v = jnp.zeros((count, LANES), F32)
     for b in range(STEPS):
-        v = v + exact(coef[b], basis[b, z // zpu, :, piece(x * zpu + lax.rem(z, zpu), LANES)].astype(F32))
+        v = v + exact(coef[b], basis[b, 0, :, piece(x, span)].astype(F32))
     gvv_v[...] = gvv
     row = lax.broadcasted_iota(jnp.int32, (ROWS, count), 0) + y * ROWS
     col = lax.broadcasted_iota(jnp.int32, (ROWS, count), 1)
@@ -414,11 +425,7 @@
         total[:, :count], gvv_v[piece(y, ROWS), :], col < row, jnp.where(row == col, F32(1.0), F32(0.0))
     )
     upd = exact(mix, v)
-    wait_for(last_recv, s3_sem.at[k, 0])
-    moved = s2_own[z // zpu, :, piece(lax.rem(z, zpu), LANES)]
-    for d in range(1, Z):
-        moved = moved + last_recv[d - 1].astype(F32)
-    upd = upd + F32(step_size) * moved
+    upd = upd + F32(step_size) * rows_of_block(k)
     upd_v[...] = upd
     send(upd_v.at[piece(o, HALF), :], upd_recv, send_sem.at[0], upd_sem, sibling)
     sq_send[0] = jnp.broadcast_to(jnp.sum(upd * upd, axis=1, keepdims=True), (ROWS, 128))
@@ -445,7 +452,6 @@
     out_ref[:, piece(o, LANES)] = upd_recv[...] * scale
 
     reduce_sent(k)
-    wait_for(last_recv, send_sem.at[7])
     wait_for(gram_recv.at[0, pl.ds(0, Y - 1)], send_sem.at[8])
     wait_for(gram_recv.at[1, pl.ds(0, X - 1)], send_sem.at[9])
     wait_for(gram_z_recv, send_sem.at[10])
@@ -457,11 +463,10 @@
 
 def on_device(data, players):
     Z = lax.axis_size("wide") // X
-    U = min(UNITS, Z)
     depth, features = data.shape
     nrows = depth * lax.axis_size("wide") * lax.axis_size("narrow")
     count = Y * ROWS
-    span = Z // U * LANES
+    span = LANES
     most = max(X, Y) - 1
     parts = 2 * depth + STEPS * count
     parts = -(-parts // 128) * 128
@@ -474,18 +479,17 @@
         out_specs=pl.BlockSpec(memory_space=pltpu.VMEM),
         scratch_shapes=[
             pltpu.VMEM((2 * depth, features // 2), BF16),
-            pltpu.VMEM((STEPS, U, count, X * span), BF16),
+            pltpu.VMEM((STEPS, Z, count, X * span), BF16),
             pltpu.VMEM((HALF, LANES), F32),
             pltpu.VMEM((STEPS, count, parts), F32),
             pltpu.VMEM((STEPS, count, parts), F32),
-            pltpu.VMEM((U, count, X * span), BF16),
-            pltpu.VMEM((U, count, X * span), BF16),
-            pltpu.VMEM((U, max(X, Y) * ROWS, span), BF16),
-            pltpu.VMEM((U, most, ROWS, span), BF16),
-            pltpu.VMEM((U, ROWS, span), F32),
-            pltpu.VMEM((U, ROWS, span), BF16),
-            pltpu.VMEM((STEPS - 1, U, Z - 1, ROWS, span), BF16),
-            pltpu.VMEM((Z - 1, ROWS, LANES), BF16),
+            pltpu.VMEM((Z, count, X * span), BF16),
+            pltpu.VMEM((Z, count, X * span), BF16),
+            pltpu.VMEM((Z, max(X, Y) * ROWS, span), BF16),
+            pltpu.VMEM((Z, most, ROWS, span), BF16),
+            pltpu.VMEM((ROWS, span), F32),
+            pltpu.VMEM((Z - 1, ROWS, span), BF16),
+            pltpu.VMEM((STEPS, Z - 1, ROWS, span), BF16),
             pltpu.VMEM((3, count, 128), F32),
             pltpu.VMEM((2, most, ROWS, 128), F32),
             pltpu.VMEM((Z - 1, ROWS, 128), F32),
@@ -502,12 +506,12 @@
             dma((11,)),
             dma,
             dma((STEPS,)),
-            dma,
-            dma((STEPS, U)),
-            dma((STEPS, U)),
-            dma((STEPS, U)),
-            dma((STEPS, U)),
-            dma((STEPS, U)),
+            dma((STEPS, Z)),
+            dma((STEPS, Z)),
+            dma((STEPS, Z)),
+            dma((STEPS,)),
+            dma((STEPS, Z)),
+            dma((STEPS, Z)),
             dma((3,)),
             dma((3,)),
             dma,

time: 133 us -> 120 us (0.902)
  Pallas kernels: 132 us -> 119 us
    pallas_call x1, Pallas kernels: 132 us -> 119 us  [on_device(): pl.pallas_call(functools.partial(kernel, Z, nrows), out_shape=jax.ShapeDt...]
where the time goes in v3:
time: 120 us
  Pallas kernels  119 us (99%)
  local copies, waits for them, and re-layouts  1.32 us (1%)
    pallas_call x1, Pallas kernels, on_device(): pl.pallas_call(functools.partial(kernel, Z, nrows), out_shape=jax.ShapeDt...  119 us

profile of v3, /device:TPU:1, one launch (start us, length us, event | category | flops | bytes accessed | tf_op | source)
XLA Modules:
  0.0 120.0 jit_solution(447550751571198070)
XLA Ops:
  0.0 0.0 copy-start
  0.0 0.7 copy-done
  0.7 118.7 %shard_map.28 = f32[8,512]{1,0:T(8,128)S(1)} custom-call(bf16[256,16384]{1,0:T(8,128)(2,1)} %data_hbm.1, f32[8,512]{1,0:T(8,128)S(1)} %copy-done), custom_call_target="tpu_custom_call" | custom-call | flops 3221225472 | bytes 8388608 | tf_op jit(solution)/shard_map/pallas_call | solution.py:475
  119.4 0.6 copy.4
Async XLA Ops:
  0.0 0.7 copy-start

commit v4 on v3

--- a/solution.py
+++ b/solution.py
@@ -30,6 +30,10 @@
 
 def nt(a, b):
     return lax.dot_general(a, b, (((1,), (1,)), ((), ())), preferred_element_type=F32)
+
+
+def order(n):
+    return sorted(range(1, n), key=lambda d: -min(d, n - d))
 
 
 def kernel(
@@ -117,13 +121,12 @@
         pltpu.make_async_copy(data_hbm.at[:, piece(q * 2 + c, LANES)], data_v.at[place(q)], load_sem).start()
         return carry
 
-    lax.fori_loop(0, Z * X, load, 0)
 
     barrier = pltpu.get_barrier_semaphore()
-    peers = [sibling]
+    peers = [at_z(d) for d in far[:-1]]
     peers += [at_x(d) for d in range(1, X)]
     peers += [at_y(d) for d in range(1, Y)]
-    peers += [at_z(d) for d in range(1, Z)]
+    peers += [sibling]
     for peer in peers:
         pl.semaphore_signal(barrier, inc=1, device_id=peer, device_id_type=MESH)
     pl.semaphore_wait(barrier, len(peers))
@@ -162,22 +165,22 @@
             wait_for(z_recv.at[0, 0], za_sem.at[j, u])
         part = basis.at[j, u, piece(y, ROWS), piece(x, span)]
         if u % 2 == 0:
-            for d in range(1, Y):
+            for d in order(Y):
                 send(part, part, send_sem.at[2], s4_sem.at[j, u], at_y(d))
         else:
-            for d in range(1, X):
+            for d in order(X):
                 send(part, part, send_sem.at[2], s4_sem.at[j, u], at_x(d))
 
     def fifth(j, u):
         if u % 2 == 0:
             wait_for(s2_recv.at[u, pl.ds(0, Y - 1)], s4_sem.at[j, u])
             part = basis.at[j, u, :, piece(x, span)]
-            for d in range(1, X):
+            for d in order(X):
                 send(part, part, send_sem.at[3], s5_sem.at[j, u], at_x(d))
         else:
             wait_for(s2_recv.at[u, pl.ds(0, X - 1)], s4_sem.at[j, u])
             part = basis.at[j, u, piece(y, ROWS), :]
-            for d in range(1, Y):
+            for d in order(Y):
                 send(part, part, send_sem.at[3], s5_sem.at[j, u], at_y(d))
 
     def contract(j, u):
@@ -209,9 +212,13 @@
 
     def gather(j):
         fourth(j, 0)
+        if j == 0:
+            lax.fori_loop(0, Z * X, swap, 0)
         for u in near[1:3]:
             fourth(j, u)
         fifth(j, 0)
+        if j == 0:
+            lax.fori_loop(0, Z * X, load, 0)
         for u in near[3:]:
             fourth(j, u)
         for u in near[1:]:
@@ -236,7 +243,7 @@
             r = jnp.dot(pt, data_v[:, at : at + span], preferred_element_type=F32)
             s1_send[u, :, xq * span : (xq + 1) * span] = r.astype(BF16)
         if u % 2 == 0:
-            for d in range(1, X):
+            for d in order(X):
                 send(
                     s1_send.at[u, :, piece(lax.rem(x + d, X), span)],
                     s1_recv.at[u, :, pl.ds((d - 1) * span, span)],
@@ -245,7 +252,7 @@
                     at_x(d),
                 )
         else:
-            for d in range(1, Y):
+            for d in order(Y):
                 send(
                     s1_send.at[u, piece(lax.rem(y + d, Y), ROWS), :],
                     s1_recv.at[u, pl.ds((d - 1) * ROWS, ROWS), :],
@@ -261,7 +268,7 @@
             for d in range(1, X):
                 total = total + s1_recv[u, :, (d - 1) * span : d * span].astype(F32)
             s2_send[u] = total.astype(BF16)
-            for d in range(1, Y):
+            for d in order(Y):
                 send(
                     s2_send.at[u, piece(lax.rem(y + d, Y), ROWS), :],
                     s2_recv.at[u, d - 1],
@@ -276,7 +283,7 @@
                 total = total + s1_recv[u, (d - 1) * ROWS : d * ROWS, :].astype(F32)
             for xq in range(X):
                 s2_send[u, xq * ROWS : (xq + 1) * ROWS, :] = total[:, xq * span : (xq + 1) * span].astype(BF16)
-            for d in range(1, X):
+            for d in order(X):
                 send(
                     s2_send.at[u, piece(lax.rem(x + d, X), ROWS), :],
                     s2_recv.at[u, d - 1],
@@ -300,9 +307,10 @@
             send(s3_send.at[u - 1], z_recv.at[k, u - 1], send_sem.at[7], s3_sem.at[k], at_z(u))
         return total
 
-    def reduce(k, pt):
+    def reduce(k, pt, meanwhile):
         for u in far:
             first_stage(k, u, pt)
+        meanwhile()
         gather_sent(k)
         for u in far:
             second_stage(k, u)
@@ -337,20 +345,24 @@
         return diagonal * (F32(1.0) - F32(step_size) * align) - F32(step_size) * weights
 
     along_z(0)
-    lax.fori_loop(0, Z * X, swap, 0)
     gather(0)
     proj, (gvv,) = whole(0)
-    coef = [eye]
+    state = {"gvv": gvv, "coef": [eye]}
+
+    def meanwhile():
+        pass
+
     wait_for(players_recv, send_sem.at[0])
     wait_for(data_v.at[pl.ds(0, depth)], swap_send_sem)
 
     for k in range(STEPS - 1):
         pt = (proj.astype(BF16).astype(F32) * F32(1.0 / nrows)).astype(BF16)
-        reduce(k, pt)
+        reduce(k, pt, meanwhile)
         basis[k + 1, 0, piece(y, ROWS), piece(x, span)] = rows_of_block(k).astype(BF16)
         along_z(k + 1)
         gather(k + 1)
         q, inner = whole(k + 1)
+        gvv, coef = state["gvv"], state["coef"]
         gram = exact(inner[0], coef[0], ((1,), (1,)))
         for b in range(1, k + 1):
             gram = gram + exact(inner[b], coef[b], ((1,), (1,)))
@@ -363,21 +375,24 @@
         )
         scale = lax.rsqrt(length + F32(epsilon))
         proj = scale * (exact(mix, proj) + F32(step_size) * q)
-        cross = exact(mix, gram, ((1,), (1,)))
-        guu = (
-            exact(mixed, mix, ((1,), (1,)))
-            + F32(step_size) * (cross + cross.T)
-            + F32(step_size**2) * inner[k + 1]
-        )
-        gvv = scale * guu * jnp.sum(eye * scale, axis=0, keepdims=True)
-        coef = [scale * exact(mix, a) for a in coef] + [scale * F32(step_size) * eye]
+
+        def meanwhile(k=k, coef=coef, mix=mix, mixed=mixed, gram=gram, scale=scale, inner=inner):
+            cross = exact(mix, gram, ((1,), (1,)))
+            guu = (
+                exact(mixed, mix, ((1,), (1,)))
+                + F32(step_size) * (cross + cross.T)
+                + F32(step_size**2) * inner[k + 1]
+            )
+            state["gvv"] = scale * guu * jnp.sum(eye * scale, axis=0, keepdims=True)
+            state["coef"] = [scale * exact(mix, a) for a in coef] + [scale * F32(step_size) * eye]
+
         reduce_sent(k)
 
     k = STEPS - 1
     pt = (proj.astype(BF16).astype(F32) * F32(1.0 / nrows)).astype(BF16)
     gram = exact(pt.astype(F32), proj, ((1,), (1,)))
     gram_send[0] = jnp.concatenate([gram, jnp.zeros((count, 128 - count), F32)], axis=1)
-    for d in range(1, Y):
+    for d in order(Y):
         send(
             gram_send.at[0, piece(lax.rem(y + d, Y), ROWS), :],
             gram_recv.at[0, d - 1],
@@ -387,13 +402,15 @@
         )
     for u in far:
         first_stage(k, u, pt)
+    meanwhile()
+    gvv, coef = state["gvv"], state["coef"]
     gather_sent(k)
     wait_for(gram_recv.at[0, pl.ds(0, Y - 1)], gram_sem.at[0])
     total = gram_send[0, piece(y, ROWS), :]
     for d in range(1, Y):
         total = total + gram_recv[0, d - 1]
     gram_send[1, :ROWS, :] = total
-    for d in range(1, X):
+    for d in order(X):
         send(
             gram_send.at[1, pl.ds(0, ROWS)], gram_recv.at[1, d - 1], send_sem.at[9], gram_sem.at[1], at_x(d)
         )
@@ -436,7 +453,7 @@
     for d in range(1, Z):
         total = total + sq_z_recv[d - 1]
     sq_send[1] = total
-    for d in range(1, X):
+    for d in order(X):
         send(sq_send.at[1], sq_recv.at[d - 1], send_sem.at[2], sq_sem.at[1], at_x(d))
     wait_for(sq_recv, sq_sem.at[1])
     total = sq_send[1]

time: 120 us -> 119 us (level)
  Pallas kernels: 119 us -> 117 us
    pallas_call x1, Pallas kernels: 119 us -> 117 us  [on_device(): pl.pallas_call(functools.partial(kernel, Z, nrows), out_shape=jax.ShapeDt...]
where the time goes in v4:
time: 119 us
  Pallas kernels  117 us (98%)
  local copies, waits for them, and re-layouts  1.32 us (1%)
    pallas_call x1, Pallas kernels, on_device(): pl.pallas_call(functools.partial(kernel, Z, nrows), out_shape=jax.ShapeDt...  117 us

profile of v4, /device:TPU:1, one launch (start us, length us, event | category | flops | bytes accessed | tf_op | source)
XLA Modules:
  0.0 118.7 jit_solution(10748301288714169186)
XLA Ops:
  0.0 0.0 copy-start
  0.0 0.7 copy-done
  0.7 117.3 %shard_map.28 = f32[8,512]{1,0:T(8,128)S(1)} custom-call(bf16[256,16384]{1,0:T(8,128)(2,1)} %data_hbm.1, f32[8,512]{1,0:T(8,128)S(1)} %copy-done), custom_call_target="tpu_custom_call" | custom-call | flops 3221225472 | bytes 8388608 | tf_op jit(solution)/shard_map/pallas_call | solution.py:492
  118.1 0.6 copy.4
Async XLA Ops:
  0.0 0.7 copy-start
